TPU v7x, 256 devices: a whole 4x4x8 slice. The times are simulated.
256 devices in a mesh: ta: 4 (over x), ha: 8 (over z), wa: 8 (over y, core).
Axes of the slice: x: 4, y: 4, z: 8, core: 2. Of those that a mesh axis runs over, the one named last changes fastest.
Arguments:
- latents: float32 [8, 32, 32, 384], P('ta', 'ha', 'wa'), may hold values from -6 to 6
- first_gain: float32 [384], replicated, may hold values from 0.1 to 1.9
- first_kernel: float32 [384, 3, 3, 3, 384], P('wa'), may hold values from -0.0625 to 0.0625
- first_bias: float32 [384], replicated, may hold values from -3 to 3
- second_gain: float32 [384], replicated, may hold values from 0.1 to 1.9
- second_kernel: float32 [384, 3, 3, 3, 384], P('wa'), may hold values from -0.0625 to 0.0625
- second_bias: float32 [384], replicated, may hold values from -3 to 3
- attn_gain: float32 [384], replicated, may hold values from 0.1 to 1.9
- w_query: float32 [384, 384], replicated, may hold values from -2 to 2, as said below
- w_key: float32 [384, 384], replicated, may hold values from -2 to 2, as said below
- w_value: float32 [384, 384], replicated, may hold values from -0.3125 to 0.3125
- w_out: float32 [384, 384], replicated, may hold values from -0.3125 to 0.3125
- out_bias: float32 [384], replicated, may hold values from -3 to 3
Outputs:
- decoded: float32 [8, 32, 32, 384], P('ta', 'ha', 'wa')
Inputs may be any that keep to these rules, and one draw needn't show every extreme that they name: `w_query`: a dense matrix. `w_key`: a dense matrix.
All inputs are finite; a program needn't handle non-finite values.
Results may differ from a plain program's by a relative error of at most 0.00017.
Values sent between devices are 32-bit elements; how exact they have to be, the bound alone decides.
No kernel may reach another device: no remote copies, remote signals or barrier semaphores. Data moves between devices by JAX's collectives and lax.ppermute only.
A program may use at most 64 MiB of HBM per device.

v0:
```python
import math
import jax
import jax.numpy as jnp
from jax import lax
from jax.sharding import PartitionSpec as P


def from_behind(shard, axis, by):
    peers = lax.axis_size(axis)
    pairs = [(i, i + by) for i in range(peers) if 0 <= i + by < peers]
    return lax.ppermute(shard, axis, pairs)


def padded_2(cells, sides, width):
    for axis, dim in sides:
        count = lax.axis_size(axis)
        ends = count - 1
        head = lax.slice_in_dim(cells, 0, width, axis=dim)
        tail = lax.slice_in_dim(cells, cells.shape[dim] - width, cells.shape[dim], axis=dim)
        cells = jnp.concatenate(
            [
                lax.ppermute(tail, axis, [(i, (i + 1) % count) for i in range(ends)]),
                cells,
                lax.ppermute(head, axis, [((i + 1) % count, i) for i in range(ends)]),
            ],
            axis=dim,
        )
    return cells


def channel_norm(values, gain):
    return values * lax.rsqrt(jnp.mean(values * values, axis=-1, keepdims=True) + 1e-06) * gain


def causal_conv(activated, kernel, bias):
    frames = activated.shape[0]
    channels = activated.shape[3]
    out_count = kernel.shape[0]
    widened = lax.all_gather(activated, "wa", axis=2, tiled=True)
    earlier = from_behind(widened, "ta", 1)
    extended = jnp.concatenate([earlier, widened], axis=0)
    padded = padded_2(extended, (("ha", 1),), 1)
    padded = jnp.pad(padded, ((0, 0), (0, 0), (1, 1), (0, 0)))
    heights = activated.shape[1]
    widths = padded.shape[2] - 2
    row_count = frames * heights * widths
    summed = jnp.zeros((row_count, out_count), jnp.float32)
    for time_tap in range(3):
        patches = jnp.concatenate(
            [
                padded[
                    time_tap : time_tap + frames,
                    row_tap : row_tap + heights,
                    col_tap : col_tap + widths,
                ].reshape(row_count, channels)
                for row_tap in range(3)
                for col_tap in range(3)
            ],
            axis=1,
        )
        tap_kernel = kernel[:, time_tap].reshape(out_count, 9 * channels)
        summed = summed + lax.dot_general(
            patches,
            tap_kernel,
            (((1,), (1,)), ((), ())),
            precision=lax.Precision.HIGHEST,
            preferred_element_type=jnp.float32,
        )
    strip = summed.reshape(frames, heights, widths, out_count)
    owned = lax.all_to_all(strip, "wa", split_axis=2, concat_axis=3, tiled=True)
    return owned + bias


def absorb_keys(carry, queries, key_piece, value_piece, scale):
    top, denom, accum = carry
    scores = jnp.einsum("fqc,fkc->fqk", queries, key_piece, precision=lax.Precision.HIGHEST) * scale
    new_top = jnp.maximum(top, jnp.max(scores, axis=-1))
    weights = jnp.exp(scores - new_top[..., None])
    denom = jnp.sum(weights, axis=-1)
    accum = jnp.einsum("fqk,fkc->fqc", weights, value_piece, precision=lax.Precision.HIGHEST)
    return (new_top, denom, accum)


def per_device(
    latents,
    first_gain,
    first_kernel,
    first_bias,
    second_gain,
    second_kernel,
    second_bias,
    attn_gain,
    w_query,
    w_key,
    w_value,
    w_out,
    out_bias,
):
    inner = causal_conv(jax.nn.silu(channel_norm(latents, first_gain)), first_kernel, first_bias)
    blocked = latents + causal_conv(
        jax.nn.silu(channel_norm(inner, second_gain)), second_kernel, second_bias
    )
    frames, heights, widths, channels = blocked.shape
    cell_count = heights * widths
    normed_rows = channel_norm(blocked, attn_gain).reshape(frames * cell_count, channels)
    queries = jnp.dot(
        normed_rows, w_query, precision=lax.Precision.HIGHEST, preferred_element_type=jnp.float32
    ).reshape(frames, cell_count, channels)
    scale = 1.0 / math.sqrt(channels)
    start_state = (
        jnp.full((frames, cell_count), -1e30, jnp.float32),
        jnp.zeros((frames, cell_count), jnp.float32),
        jnp.zeros((frames, cell_count, channels), jnp.float32),
    )
    keys = jnp.dot(
        normed_rows, w_key, precision=lax.Precision.HIGHEST, preferred_element_type=jnp.float32
    ).reshape(frames, cell_count, channels)
    values = jnp.dot(
        normed_rows, w_value, precision=lax.Precision.HIGHEST, preferred_element_type=jnp.float32
    ).reshape(frames, cell_count, channels)
    top, denom, accum = absorb_keys(
        start_state,
        queries,
        lax.all_gather(keys, ("ha", "wa"), axis=1, tiled=True),
        lax.all_gather(values, ("ha", "wa"), axis=1, tiled=True),
        scale,
    )
    mixed = accum / denom[..., None]
    projected = (
        jnp.dot(
            mixed.reshape(frames * cell_count, channels),
            w_out,
            precision=lax.Precision.HIGHEST,
            preferred_element_type=jnp.float32,
        )
        + out_bias
    )
    return blocked + projected.reshape(frames, heights, widths, channels)


def solution(mesh):
    in_specs = (
        P("ta", "ha", "wa", None),
        P(),
        P("wa", None, None, None, None),
        P(),
        P(),
        P("wa", None, None, None, None),
        P(),
        P(),
        P(),
        P(),
        P(),
        P(),
        P(),
    )
    out_specs = P("ta", "ha", "wa", None)
    return jax.shard_map(
        per_device, mesh=mesh, in_specs=in_specs, out_specs=out_specs, check_vma=False
    )
```

profile of v0, /device:TPU:1, one launch (start us, length us, event | category | flops | bytes accessed | tf_op | source)
XLA Modules:
  0.0 315.1 jit_solution(18345777338632848029)
XLA Ops:
  8.5 16.1 %all_gather.12 = f32[2,4,32,384]{3,1,0,2:T(4,128)S(1)} all-gather(f32[2,4,4,384]{3,1,0,2:T(4,128)S(1)} %copy.50), channel_id=1, replica_groups=mesh['ta'=4,'ha'=8,'wa'=8] {'wa'}, dimensions={2}, use_global_device_ids=true | all-gather | bytes 442368 | tf_op jit(solution)/shard_map/all_gather | solution.py:39
  24.7 1.9 collective-permute-start
  26.6 8.3 %collective-permute-done = f32[2,4,32,384]{3,2,1,0:T(8,128)S(1)} collective-permute-done((f32[2,4,32,384]{3,2,1,0:T(8,128)S(1)}, f32[2,4,32,384]{3,2,1,0:T(8,128)S(1)}, u32[]{:S(2)}, u32[]{:S(2)}) %collective-permute-start) | collective-permute-done | bytes 393248 | tf_op jit(solution)/shard_map/ppermute | solution.py:11
  35.8 3.5 %collective-permute-start.1 = (f32[4,1,32,384]{3,2,1,0:T(8,128)}, f32[4,1,32,384]{3,2,1,0:T(8,128)S(1)}, u32[]{:S(2)}, u32[]{:S(2)}) collective-permute-start(f32[4,1,32,384]{3,2,1,0:T(8,128)} %get-tuple-element.71), channel_id=1, source_target_pairs={{0,8},{8,16},{16,24},{24,32},{32,40},{40,48},{48,56},{1,9},{9,17},... | collective-permute-start | bytes 589832 | tf_op jit(solution)/shard_map/ppermute | solution.py:22
  39.4 1.3 collective-permute-start.2
  42.6 1.4 copy.53
  44.1 1.2 reshape_squeeze.18
  45.3 1.4 copy.56
  50.0 1.4 pad_maximum_fusion.2
  52.2 3.1 fusion.24
  55.4 3.1 convolution_add_fusion.4
  58.6 3.1 convolution_add_fusion.3
  62.7 5.0 %all-to-all-start = ((f32[8,1,1536]{2,1,0:T(1,128)}), f32[8,1,1536]{2,1,0:T(1,128)S(1)}, u32[]{:S(2)}, u32[]{:S(2)}) async-start(f32[8,1,1536]{2,1,0:T(1,128)} %reshape.280), calls=%async_computation | async-start | bytes 98304 | tf_op jit(solution)/shard_map/all_to_all | solution.py:70
  67.8 4.7 %all-to-all-done = f32[8,1,1536]{2,1,0:T(1,128)S(1)} async-done(((f32[8,1,1536]{2,1,0:T(1,128)}), f32[8,1,1536]{2,1,0:T(1,128)S(1)}, u32[]{:S(2)}, u32[]{:S(2)}) %all-to-all-start) | async-done | bytes 49184 | tf_op jit(solution)/shard_map/all_to_all | solution.py:70
  74.4 13.6 %all_gather.13 = f32[2,4,32,384]{3,1,0,2:T(4,128)S(1)} all-gather(f32[2,4,4,384]{3,1,0,2:T(4,128)S(1)} %copy.61), channel_id=1, replica_groups=mesh['ta'=4,'ha'=8,'wa'=8] {'wa'}, dimensions={2}, use_global_device_ids=true | all-gather | bytes 442368 | tf_op jit(solution)/shard_map/all_gather | solution.py:39
  88.1 4.1 %collective-permute-start.3 = (f32[2,4,32,384]{3,2,1,0:T(8,128)S(1)}, f32[2,4,32,384]{3,2,1,0:T(8,128)S(1)}, u32[]{:S(2)}, u32[]{:S(2)}) collective-permute-start(f32[2,4,32,384]{3,2,1,0:T(8,128)S(1)} %copy.62), channel_id=1, source_target_pairs={{0,64},{64,128},{128,192},{1,65},{65,129},{129,193},{2,66},{66,130... | collective-permute-start | bytes 1179656 | tf_op jit(solution)/shard_map/ppermute | solution.py:11
  92.2 8.3 %collective-permute-done.3 = f32[2,4,32,384]{3,2,1,0:T(8,128)S(1)} collective-permute-done((f32[2,4,32,384]{3,2,1,0:T(8,128)S(1)}, f32[2,4,32,384]{3,2,1,0:T(8,128)S(1)}, u32[]{:S(2)}, u32[]{:S(2)}) %collective-permute-start.3) | collective-permute-done | bytes 393248 | tf_op jit(solution)/shard_map/ppermute | solution.py:11
  101.4 4.3 %collective-permute-start.4 = (f32[4,1,32,384]{3,2,1,0:T(8,128)}, f32[4,1,32,384]{3,2,1,0:T(8,128)S(1)}, u32[]{:S(2)}, u32[]{:S(2)}) collective-permute-start(f32[4,1,32,384]{3,2,1,0:T(8,128)} %get-tuple-element.65), channel_id=1, source_target_pairs={{0,8},{8,16},{16,24},{24,32},{32,40},{40,48},{48,56},{1,9},{9,17},... | collective-permute-start | bytes 589832 | tf_op jit(solution)/shard_map/ppermute | solution.py:22
  105.7 1.3 collective-permute-start.5
  107.0 2.7 fusion.17
  110.4 1.4 copy.64
  111.9 1.2 reshape_squeeze.21
  113.1 1.4 copy.67
  117.8 1.4 pad_maximum_fusion
  120.1 3.1 fusion.25
  123.2 3.1 convolution_add_fusion.2
  126.4 3.1 convolution_add_fusion.1
  130.0 8.6 %all_to_all.36 = f32[8,1,1536]{2,1,0:T(1,128)S(1)} all-to-all(f32[8,1,1536]{2,1,0:T(1,128)S(1)} %reshape.282), channel_id=1, replica_groups=mesh['ta'=4,'ha'=8,'wa'=8] {'wa'}, dimensions={0} | all-to-all | bytes 98304 | tf_op jit(solution)/shard_map/all_to_all | solution.py:70
  142.6 82.5 %all-gather.3.cloned.1.call-done = f32[2,1024,384]{2,1,0:T(8,128)} async-done(((f32[2,16,384]{2,1,0:T(8,128)}), f32[2,1024,384]{2,1,0:T(8,128)}) %all-gather.3.cloned.1.call-update) | async-done | bytes 3145744 | tf_op jit(solution)/shard_map/all_gather | solution.py:124
  225.1 4.6 %fusion.23 = (f32[2,16]{1,0:T(2,128)S(1)}, f32[2,16,1024]{2,1,0:T(8,128)S(1)}) fusion(f32[2,16,384]{2,1,0:T(8,128)S(1)} %fusion.5, f32[2,1024,384]{2,1,0:T(8,128)} %all-gather.3.cloned.1.call-done), kind=kOutput, calls=%fused_computation.126 | convolution fusion | flops 151060448 | bytes 3326080 | tf_op jit(solution)/shard_map/fqc,fkc->fqk/dot_general | solution.py:76
  229.9 73.7 %all-gather.5.cloned.1.call-done = f32[2,1024,384]{2,1,0:T(8,128)} async-done(((f32[2,16,384]{2,1,0:T(8,128)}), f32[2,1024,384]{2,1,0:T(8,128)}) %all-gather.5.cloned.1.call-update) | async-done | bytes 3145744 | tf_op jit(solution)/shard_map/all_gather | solution.py:125
  303.6 3.5 %convolution_divide_fusion = f32[2,16,384]{2,1,0:T(8,128)S(1)} fusion(f32[2,1024,384]{2,1,0:T(8,128)} %all-gather.5.cloned.1.call-done, f32[2,16,1024]{2,1,0:T(8,128)S(1)} %get-tuple-element.74, f32[2,16]{1,0:T(2,128)S(1)} %broadcast_maximum_fusion, f32[2,16]{1,0:T(2,128)S(1)} %fusion.15), kind=kOutput, calls=%fused_computation.17 | convolution fusion | flops 151040000 | bytes 3326208 | tf_op jit(solution)/shard_map/fqk,fkc->fqc/dot_general | solution.py:80
  (157 shorter events, 22.8 us)
Async XLA Ops:
  6.5 133.4 %copy-start = (f32[384,384]{1,0:T(8,128)S(1)}, f32[384,384]{1,0:T(8,128)}, u32[]{:S(2)}) copy-start(f32[384,384]{1,0:T(8,128)} %param.22) | copy-start | bytes 1769476
  6.5 34.1 %copy-start.5 = (f32[48,3,3,3,384]{4,0,3,2,1:T(8,128)S(1)}, f32[48,3,3,3,384]{4,0,3,2,1:T(8,128)}, u32[]{:S(2)}) copy-start(f32[48,3,3,3,384]{4,0,3,2,1:T(8,128)} %param.15) | copy-start | bytes 5971972
  24.7 14.7 %copy-start.6 = (f32[2,4,32,384]{3,2,1,0:T(8,128)}, f32[2,4,32,384]{3,2,1,0:T(8,128)S(1)}, u32[]{:S(2)}) copy-start(f32[2,4,32,384]{3,2,1,0:T(8,128)S(1)} %copy.51) | copy-start | bytes 1179652
  24.7 10.3 %collective-permute-start = (f32[2,4,32,384]{3,2,1,0:T(8,128)S(1)}, f32[2,4,32,384]{3,2,1,0:T(8,128)S(1)}, u32[]{:S(2)}, u32[]{:S(2)}) collective-permute-start(f32[2,4,32,384]{3,2,1,0:T(8,128)S(1)} %copy.51), channel_id=1, source_target_pairs={{0,64},{64,128},{128,192},{1,65},{65,129},{129,193},{2,66},{66,130... | collective-permute-start | bytes 1179656 | tf_op jit(solution)/shard_map/ppermute | solution.py:11
  35.8 12.1 %collective-permute-start.1 = (f32[4,1,32,384]{3,2,1,0:T(8,128)}, f32[4,1,32,384]{3,2,1,0:T(8,128)S(1)}, u32[]{:S(2)}, u32[]{:S(2)}) collective-permute-start(f32[4,1,32,384]{3,2,1,0:T(8,128)} %get-tuple-element.71), channel_id=1, source_target_pairs={{0,8},{8,16},{16,24},{24,32},{32,40},{40,48},{48,56},{1,9},{9,17},... | collective-permute-start | bytes 589832 | tf_op jit(solution)/shard_map/ppermute | solution.py:22
  39.4 8.6 %collective-permute-start.2 = (f32[4,1,32,384]{3,2,1,0:T(8,128)}, f32[4,1,32,384]{3,2,1,0:T(8,128)}, u32[]{:S(2)}, u32[]{:S(2)}) collective-permute-start(f32[4,1,32,384]{3,2,1,0:T(8,128)} %get-tuple-element.72), channel_id=1, source_target_pairs={{8,0},{16,8},{24,16},{32,24},{40,32},{48,40},{56,48},{9,1},{17,9},... | collective-permute-start | bytes 589832 | tf_op jit(solution)/shard_map/ppermute | solution.py:24
  50.0 1.5 copy-start.7
  52.1 3.3 %copy-start.1 = (f32[48,3456]{1,0:T(8,128)S(1)}, f32[48,3456]{1,0:T(8,128)}, u32[]{:S(2)}) copy-start(f32[48,3456]{1,0:T(8,128)} %reshape_squeeze.18) | copy-start | bytes 1990660
  52.2 6.3 %copy-start.3 = (f32[48,3456]{1,0:T(8,128)S(1)}, f32[48,3456]{1,0:T(8,128)}, u32[]{:S(2)}) copy-start(f32[48,3456]{1,0:T(8,128)} %reshape_squeeze.20) | copy-start | bytes 1990660
  58.6 9.2 %copy-start.14 = (f32[384]{0:T(512)S(1)}, f32[384]{0:T(512)}, u32[]{:S(2)}) copy-start(f32[384]{0:T(512)} %param.16) | copy-start | bytes 4612
  58.6 15.7 %copy-start.18 = (f32[384]{0:T(512)S(1)}, f32[384]{0:T(512)}, u32[]{:S(2)}) copy-start(f32[384]{0:T(512)} %param.17) | copy-start | bytes 4612
  62.7 9.8 %all-to-all-start = ((f32[8,1,1536]{2,1,0:T(1,128)}), f32[8,1,1536]{2,1,0:T(1,128)S(1)}, u32[]{:S(2)}, u32[]{:S(2)}) async-start(f32[8,1,1536]{2,1,0:T(1,128)} %reshape.280), calls=%async_computation | async-start | bytes 98304 | tf_op jit(solution)/shard_map/all_to_all | solution.py:70
  67.7 157.4 %all-gather.3.cloned.1.call-start = ((), (), s32[]{:S(2)}) async-start(), calls=%async_computation.2 | async-start | bytes 3194880 | tf_op jit(solution)/shard_map/all_gather | solution.py:124
  88.1 17.6 %copy-start.8 = (f32[2,4,32,384]{3,2,1,0:T(8,128)}, f32[2,4,32,384]{3,2,1,0:T(8,128)S(1)}, u32[]{:S(2)}) copy-start(f32[2,4,32,384]{3,2,1,0:T(8,128)S(1)} %copy.62) | copy-start | bytes 1179652
  88.1 12.5 %collective-permute-start.3 = (f32[2,4,32,384]{3,2,1,0:T(8,128)S(1)}, f32[2,4,32,384]{3,2,1,0:T(8,128)S(1)}, u32[]{:S(2)}, u32[]{:S(2)}) collective-permute-start(f32[2,4,32,384]{3,2,1,0:T(8,128)S(1)} %copy.62), channel_id=1, source_target_pairs={{0,64},{64,128},{128,192},{1,65},{65,129},{129,193},{2,66},{66,130... | collective-permute-start | bytes 1179656 | tf_op jit(solution)/shard_map/ppermute | solution.py:11
  101.4 14.3 %collective-permute-start.4 = (f32[4,1,32,384]{3,2,1,0:T(8,128)}, f32[4,1,32,384]{3,2,1,0:T(8,128)S(1)}, u32[]{:S(2)}, u32[]{:S(2)}) collective-permute-start(f32[4,1,32,384]{3,2,1,0:T(8,128)} %get-tuple-element.65), channel_id=1, source_target_pairs={{0,8},{8,16},{16,24},{24,32},{32,40},{40,48},{48,56},{1,9},{9,17},... | collective-permute-start | bytes 589832 | tf_op jit(solution)/shard_map/ppermute | solution.py:22
  105.7 10.0 %collective-permute-start.5 = (f32[4,1,32,384]{3,2,1,0:T(8,128)}, f32[4,1,32,384]{3,2,1,0:T(8,128)}, u32[]{:S(2)}, u32[]{:S(2)}) collective-permute-start(f32[4,1,32,384]{3,2,1,0:T(8,128)} %get-tuple-element.66), channel_id=1, source_target_pairs={{8,0},{16,8},{24,16},{32,24},{40,32},{48,40},{56,48},{9,1},{17,9},... | collective-permute-start | bytes 589832 | tf_op jit(solution)/shard_map/ppermute | solution.py:24
  117.8 1.5 copy-start.9
  119.9 3.3 %copy-start.2 = (f32[48,3456]{1,0:T(8,128)S(1)}, f32[48,3456]{1,0:T(8,128)}, u32[]{:S(2)}) copy-start(f32[48,3456]{1,0:T(8,128)} %reshape_squeeze.21) | copy-start | bytes 1990660
  120.1 6.3 %copy-start.4 = (f32[48,3456]{1,0:T(8,128)S(1)}, f32[48,3456]{1,0:T(8,128)}, u32[]{:S(2)}) copy-start(f32[48,3456]{1,0:T(8,128)} %reshape_squeeze.23) | copy-start | bytes 1990660
  126.4 13.3 %copy-start.13 = (f32[2,4,4,384]{3,2,1,0:T(4,128)S(1)}, f32[2,4,4,384]{3,2,1,0:T(4,128)}, u32[]{:S(2)}) copy-start(f32[2,4,4,384]{3,2,1,0:T(4,128)} %param.13) | copy-start | bytes 147460
  126.4 13.3 %copy-start.15 = (f32[384]{0:T(512)S(1)}, f32[384]{0:T(512)}, u32[]{:S(2)}) copy-start(f32[384]{0:T(512)} %param.19) | copy-start | bytes 4612
  126.4 13.4 %copy-start.17 = (f32[384]{0:T(512)S(1)}, f32[384]{0:T(512)}, u32[]{:S(2)}) copy-start(f32[384]{0:T(512)} %param.20) | copy-start | bytes 4612
  126.4 14.6 %copy-start.10 = (f32[384,384]{1,0:T(8,128)S(1)}, f32[384,384]{1,0:T(8,128)}, u32[]{:S(2)}) copy-start(f32[384,384]{1,0:T(8,128)} %param.23) | copy-start | bytes 1769476
  126.4 15.7 %copy-start.11 = (f32[384,384]{1,0:T(8,128)S(1)}, f32[384,384]{1,0:T(8,128)}, u32[]{:S(2)}) copy-start(f32[384,384]{1,0:T(8,128)} %param.21) | copy-start | bytes 1769476
  141.0 162.6 %all-gather.5.cloned.1.call-start = ((), (), s32[]{:S(2)}) async-start(), calls=%async_computation.3 | async-start | bytes 3194880 | tf_op jit(solution)/shard_map/all_gather | solution.py:125
  142.6 164.6 %copy-start.12 = (f32[384,384]{1,0:T(8,128)S(1)}, f32[384,384]{1,0:T(8,128)}, u32[]{:S(2)}) copy-start(f32[384,384]{1,0:T(8,128)} %param.24) | copy-start | bytes 1769476
  142.6 164.5 %copy-start.16 = (f32[384]{0:T(512)S(1)}, f32[384]{0:T(512)}, u32[]{:S(2)}) copy-start(f32[384]{0:T(512)} %param.25) | copy-start | bytes 4612
Sparse Core Ops, SparseCore 0:
  141.1 83.9 all-gather.2
  227.8 75.7 all-gather.4
where the time goes:
time: 316 us; the launch traced here: 315 us
  waiting for transfers between devices  178 us (56%)
  blocking collectives  38.2 us (12%)
  matrix products  29.9 us (9%)
  local copies, waits for them, and re-layouts  23.7 us (8%)
  starting transfers between devices  21.5 us (7%)
  between operations  14.5 us (5%)
  other arithmetic  9.67 us (3%)
    all_gather x1, waiting for transfers between devices, per_device(): lax.all_gather(keys, ('ha', 'wa'), axis=1, tiled=True)  82.5 us
    all_gather x1, waiting for transfers between devices, per_device(): lax.all_gather(values, ('ha', 'wa'), axis=1, tiled=True)  73.7 us
    all_gather x2, blocking collectives, causal_conv(): widened = lax.all_gather(activated, 'wa', axis=2, tiled=True)  29.6 us
    dot_general x6, matrix products, causal_conv(): lax.dot_general(patches, tap_kernel, (((1,), (1,)), ((), ())), precision=...  18.8 us
    ppermute x2, waiting for transfers between devices, from_behind(): return lax.ppermute(shard, axis, pairs)  16.6 us
    slice x8, local copies, waits for them, and re-layouts, causal_conv(): tap_kernel = kernel[:, time_tap].reshape(out_count, 9 * channels)  10.4 us
    all_to_all x1, blocking collectives, causal_conv(): owned = lax.all_to_all(strip, 'wa', split_axis=2, concat_axis=3, tiled=True)  8.61 us
    ppermute x2, starting transfers between devices, padded_2(): lax.ppermute(tail, axis, [(i, (i + 1) % count) for i in range(ends)])  7.81 us
  transfers between devices with their start and end apart: 9, of which 5 were waited for; matrix products, arithmetic and copies ran while one was open for 7% of the time, Pallas kernels for 0%

commit v1 on v0

--- a/solution.py
+++ b/solution.py
@@ -3,6 +3,18 @@
 import jax.numpy as jnp
 from jax import lax
 from jax.sharding import PartitionSpec as P
+
+
+def in_blocks(x, dim, size):
+    shape = x.shape
+    blocks = x.reshape(*shape[:dim], size, shape[dim] // size, *shape[dim + 1 :])
+    return jnp.moveaxis(blocks, dim, 0)
+
+
+def laid_out(blocks, dim):
+    blocks = jnp.moveaxis(blocks, 0, dim)
+    shape = blocks.shape
+    return blocks.reshape(*shape[:dim], shape[dim] * shape[dim + 1], *shape[dim + 2 :])
 
 
 def from_behind(shard, axis, by):
@@ -67,7 +79,16 @@
             preferred_element_type=jnp.float32,
         )
     strip = summed.reshape(frames, heights, widths, out_count)
-    owned = lax.all_to_all(strip, "wa", split_axis=2, concat_axis=3, tiled=True)
+    count_2, index = (lax.axis_size("wa"), lax.axis_index("wa"))
+    blocks = in_blocks(strip, 2, count_2)
+    outs = [blocks[index]]
+    for turn in range(1, count_2):
+        sent = blocks[(index + turn) % count_2]
+        outs.append(
+            lax.ppermute(sent, "wa", [(i_2, (i_2 + turn) % count_2) for i_2 in range(count_2)])
+        )
+    blocks = jnp.stack(outs)[(index - jnp.arange(count_2)) % count_2]
+    owned = laid_out(blocks, 3)
     return owned + bias
 
 

time: 316 us -> 321 us (1.016); the launches traced: 315 us -> 317 us
  starting transfers between devices: 21.5 us -> 35 us
  blocking collectives: 38.2 us -> 29.3 us
  other arithmetic: 9.67 us -> 6.02 us
    ppermute x0 -> x14, starting transfers between devices: none -> 17.9 us  [causal_conv(): lax.ppermute(sent, 'wa', [(i_2, (i_2 + turn) % count_2) for i_2 in range(...]
    all_to_all x1 -> x0, blocking collectives: 8.61 us -> none  [causal_conv(): owned = lax.all_to_all(strip, 'wa', split_axis=2, concat_axis=3, tiled=True)]
    ppermute x0 -> x14, waiting for transfers between devices: none -> 5.46 us  [causal_conv(): lax.ppermute(sent, 'wa', [(i_2, (i_2 + turn) % count_2) for i_2 in range(...]
    ppermute x2, waiting for transfers between devices: 16.6 us -> 11.5 us  [from_behind(): return lax.ppermute(shard, axis, pairs)]
    all_to_all x1 -> x0, starting transfers between devices: 5 us -> none  [causal_conv(): owned = lax.all_to_all(strip, 'wa', split_axis=2, concat_axis=3, tiled=True)]
    all_to_all x1 -> x0, waiting for transfers between devices: 4.7 us -> none  [causal_conv(): owned = lax.all_to_all(strip, 'wa', split_axis=2, concat_axis=3, tiled=True)]
    ppermute x2, waiting for transfers between devices: 0.01 us -> 4.19 us  [padded_2(): lax.ppermute(head, axis, [((i + 1) % count, i) for i in range(ends)])]
  transfers between devices with their start and end apart: 9 -> 22, of which waited for: 5 -> 12; matrix products, arithmetic and copies ran while one was open for 7% -> 6% of each run, Pallas kernels for 0% -> 0%
where the time goes in v1:
time: 321 us; the launch traced here: 317 us
  waiting for transfers between devices  177 us (55%)
  starting transfers between devices  35 us (11%)
  matrix products  29.9 us (9%)
  blocking collectives  29.3 us (9%)
  local copies, waits for them, and re-layouts  24.4 us (8%)
  between operations  14.7 us (5%)
  other arithmetic  6.02 us (2%)
    all_gather x1, waiting for transfers between devices, per_device(): lax.all_gather(keys, ('ha', 'wa'), axis=1, tiled=True)  81 us
    all_gather x1, waiting for transfers between devices, per_device(): lax.all_gather(values, ('ha', 'wa'), axis=1, tiled=True)  73.7 us
    all_gather x2, blocking collectives, causal_conv(): widened = lax.all_gather(activated, 'wa', axis=2, tiled=True)  29.3 us
    dot_general x6, matrix products, causal_conv(): lax.dot_general(patches, tap_kernel, (((1,), (1,)), ((), ())), precision=...  18.8 us
    ppermute x14, starting transfers between devices, causal_conv(): lax.ppermute(sent, 'wa', [(i_2, (i_2 + turn) % count_2) for i_2 in range(...  17.9 us
    ppermute x2, waiting for transfers between devices, from_behind(): return lax.ppermute(shard, axis, pairs)  11.5 us
    slice x8, local copies, waits for them, and re-layouts, causal_conv(): tap_kernel = kernel[:, time_tap].reshape(out_count, 9 * channels)  8.55 us
    ppermute x2, starting transfers between devices, padded_2(): lax.ppermute(tail, axis, [(i, (i + 1) % count) for i in range(ends)])  7.1 us
  transfers between devices with their start and end apart: 22, of which 12 were waited for; matrix products, arithmetic and copies ran while one was open for 6% of the time, Pallas kernels for 0%

profile of v1, /device:TPU:1, one launch (start us, length us, event | category | flops | bytes accessed | tf_op | source)
XLA Modules:
  0.0 316.5 jit_solution(2892412753452799097)
XLA Ops:
  8.4 16.1 %all_gather.12 = f32[2,4,32,384]{3,1,0,2:T(4,128)S(1)} all-gather(f32[2,4,4,384]{3,1,0,2:T(4,128)S(1)} %copy.44), channel_id=1, replica_groups=mesh['ta'=4,'ha'=8,'wa'=8] {'wa'}, dimensions={2}, use_global_device_ids=true | all-gather | bytes 442368 | tf_op jit(solution)/shard_map/all_gather | solution.py:51
  25.3 2.7 collective-permute-start
  28.0 1.6 fusion.20
  32.7 3.2 %collective-permute-done = f32[2,4,32,384]{3,2,1,0:T(8,128)} collective-permute-done((f32[2,4,32,384]{3,2,1,0:T(8,128)}, f32[2,4,32,384]{3,2,1,0:T(8,128)}, u32[]{:S(2)}, u32[]{:S(2)}) %collective-permute-start) | collective-permute-done | bytes 393248 | tf_op jit(solution)/shard_map/ppermute | solution.py:23
  37.0 3.6 %collective-permute-start.1 = (f32[4,1,32,384]{3,2,1,0:T(8,128)S(1)}, f32[4,1,32,384]{3,2,1,0:T(8,128)S(1)}, u32[]{:S(2)}, u32[]{:S(2)}) collective-permute-start(f32[4,1,32,384]{3,2,1,0:T(8,128)S(1)} %get-tuple-element.71), channel_id=1, source_target_pairs={{0,8},{8,16},{16,24},{24,32},{32,40},{40,48},{48,56},{1,9},{9,17},... | collective-permute-start | bytes 589832 | tf_op jit(solution)/shard_map/ppermute | solution.py:34
  40.6 1.8 collective-permute-start.2
  42.4 1.4 collective-permute-done.1
  43.8 4.2 %collective-permute-done.2 = f32[4,1,32,384]{3,2,1,0:T(8,128)S(1)} collective-permute-done((f32[4,1,32,384]{3,2,1,0:T(8,128)S(1)}, f32[4,1,32,384]{3,2,1,0:T(8,128)S(1)}, u32[]{:S(2)}, u32[]{:S(2)}) %collective-permute-start.2) | collective-permute-done | bytes 196640 | tf_op jit(solution)/shard_map/ppermute | solution.py:36
  50.4 3.1 fusion.26
  56.1 3.1 convolution_add_fusion.4
  59.3 3.1 convolution_add_fusion.3
  62.6 2.9 collective-permute-start.3
  65.5 2.8 collective-permute-start.5
  68.8 2.1 collective-permute-start.7
  73.6 1.4 collective-permute-done.9
  76.1 13.2 %all_gather.13 = f32[2,4,32,384]{3,1,0,2:T(4,128)S(1)} all-gather(f32[2,4,4,384]{3,1,0,2:T(4,128)S(1)} %copy.53), channel_id=1, replica_groups=mesh['ta'=4,'ha'=8,'wa'=8] {'wa'}, dimensions={2}, use_global_device_ids=true | all-gather | bytes 442368 | tf_op jit(solution)/shard_map/all_gather | solution.py:51
  89.4 4.1 %collective-permute-start.10 = (f32[2,4,32,384]{3,2,1,0:T(8,128)S(1)}, f32[2,4,32,384]{3,2,1,0:T(8,128)S(1)}, u32[]{:S(2)}, u32[]{:S(2)}) collective-permute-start(f32[2,4,32,384]{3,2,1,0:T(8,128)S(1)} %copy.54), channel_id=1, source_target_pairs={{0,64},{64,128},{128,192},{1,65},{65,129},{129,193},{2,66},{66,130... | collective-permute-start | bytes 1179656 | tf_op jit(solution)/shard_map/ppermute | solution.py:23
  93.5 8.3 %collective-permute-done.10 = f32[2,4,32,384]{3,2,1,0:T(8,128)S(1)} collective-permute-done((f32[2,4,32,384]{3,2,1,0:T(8,128)S(1)}, f32[2,4,32,384]{3,2,1,0:T(8,128)S(1)}, u32[]{:S(2)}, u32[]{:S(2)}) %collective-permute-start.10) | collective-permute-done | bytes 393248 | tf_op jit(solution)/shard_map/ppermute | solution.py:23
  102.7 3.5 %collective-permute-start.11 = (f32[4,1,32,384]{3,2,1,0:T(8,128)}, f32[4,1,32,384]{3,2,1,0:T(8,128)S(1)}, u32[]{:S(2)}, u32[]{:S(2)}) collective-permute-start(f32[4,1,32,384]{3,2,1,0:T(8,128)} %get-tuple-element.65), channel_id=1, source_target_pairs={{0,8},{8,16},{16,24},{24,32},{32,40},{40,48},{48,56},{1,9},{9,17},... | collective-permute-start | bytes 589832 | tf_op jit(solution)/shard_map/ppermute | solution.py:34
  106.3 1.5 collective-permute-start.12
  107.8 2.7 fusion.19
  111.2 1.4 copy.56
  113.8 1.4 copy.59
  120.8 3.1 fusion.27
  123.9 3.1 convolution_add_fusion.2
  127.2 3.1 convolution_add_fusion.1
  132.7 1.8 collective-permute-start.15
  135.7 2.6 collective-permute-start.17
  145.3 81.0 %all-gather.3.cloned.1.call-done = f32[2,1024,384]{2,1,0:T(8,128)} async-done(((f32[2,16,384]{2,1,0:T(8,128)}), f32[2,1024,384]{2,1,0:T(8,128)}) %all-gather.3.cloned.1.call-update) | async-done | bytes 3145744 | tf_op jit(solution)/shard_map/all_gather | solution.py:145
  226.3 4.6 %fusion.25 = (f32[2,16]{1,0:T(2,128)S(1)}, f32[2,16,1024]{2,1,0:T(8,128)S(1)}) fusion(f32[2,16,384]{2,1,0:T(8,128)S(1)} %fusion.5, f32[2,1024,384]{2,1,0:T(8,128)} %all-gather.3.cloned.1.call-done), kind=kOutput, calls=%fused_computation.165 | convolution fusion | flops 151060448 | bytes 3326080 | tf_op jit(solution)/shard_map/fqc,fkc->fqk/dot_general | solution.py:97
  231.1 73.7 %all-gather.5.cloned.1.call-done = f32[2,1024,384]{2,1,0:T(8,128)} async-done(((f32[2,16,384]{2,1,0:T(8,128)}), f32[2,1024,384]{2,1,0:T(8,128)}) %all-gather.5.cloned.1.call-update) | async-done | bytes 3145744 | tf_op jit(solution)/shard_map/all_gather | solution.py:146
  304.8 3.5 %convolution_divide_fusion = f32[2,16,384]{2,1,0:T(8,128)S(1)} fusion(f32[2,1024,384]{2,1,0:T(8,128)} %all-gather.5.cloned.1.call-done, f32[2,16,1024]{2,1,0:T(8,128)S(1)} %get-tuple-element.88, f32[2,16]{1,0:T(2,128)S(1)} %broadcast_maximum_fusion, f32[2,16]{1,0:T(2,128)S(1)} %fusion.15), kind=kOutput, calls=%fused_computation.19 | convolution fusion | flops 151040000 | bytes 3326208 | tf_op jit(solution)/shard_map/fqk,fkc->fqc/dot_general | solution.py:101
  (185 shorter events, 35.9 us)
Async XLA Ops:
  6.5 136.1 %copy-start = (f32[384,384]{1,0:T(8,128)S(1)}, f32[384,384]{1,0:T(8,128)}, u32[]{:S(2)}) copy-start(f32[384,384]{1,0:T(8,128)} %param.22) | copy-start | bytes 1769476
  6.5 219.8 %all-gather.3.cloned.1.call-start = ((), (), s32[]{:S(2)}) async-start(), calls=%async_computation | async-start | bytes 3194880 | tf_op jit(solution)/shard_map/all_gather | solution.py:145
  25.3 10.6 %collective-permute-start = (f32[2,4,32,384]{3,2,1,0:T(8,128)}, f32[2,4,32,384]{3,2,1,0:T(8,128)}, u32[]{:S(2)}, u32[]{:S(2)}) collective-permute-start(f32[2,4,32,384]{3,2,1,0:T(8,128)} %copy.45), channel_id=1, source_target_pairs={{0,64},{64,128},{128,192},{1,65},{65,129},{129,193},{2,66},{66,130... | collective-permute-start | bytes 1179656 | tf_op jit(solution)/shard_map/ppermute | solution.py:23
  37.0 6.8 %collective-permute-start.1 = (f32[4,1,32,384]{3,2,1,0:T(8,128)S(1)}, f32[4,1,32,384]{3,2,1,0:T(8,128)S(1)}, u32[]{:S(2)}, u32[]{:S(2)}) collective-permute-start(f32[4,1,32,384]{3,2,1,0:T(8,128)S(1)} %get-tuple-element.71), channel_id=1, source_target_pairs={{0,8},{8,16},{16,24},{24,32},{32,40},{40,48},{48,56},{1,9},{9,17},... | collective-permute-start | bytes 589832 | tf_op jit(solution)/shard_map/ppermute | solution.py:34
  40.6 7.4 %collective-permute-start.2 = (f32[4,1,32,384]{3,2,1,0:T(8,128)S(1)}, f32[4,1,32,384]{3,2,1,0:T(8,128)S(1)}, u32[]{:S(2)}, u32[]{:S(2)}) collective-permute-start(f32[4,1,32,384]{3,2,1,0:T(8,128)S(1)} %get-tuple-element.72), channel_id=1, source_target_pairs={{8,0},{16,8},{24,16},{32,24},{40,32},{48,40},{56,48},{9,1},{17,9},... | collective-permute-start | bytes 589832 | tf_op jit(solution)/shard_map/ppermute | solution.py:36
  59.3 16.7 %copy-start.14 = (f32[384]{0:T(512)S(1)}, f32[384]{0:T(512)}, u32[]{:S(2)}) copy-start(f32[384]{0:T(512)} %param.17) | copy-start | bytes 4612
  62.6 8.4 %collective-permute-start.3 = (f32[2,4,4,48]{3,2,1,0:T(4,128)S(1)}, f32[2,4,4,48]{3,2,1,0:T(4,128)S(1)}, u32[]{:S(2)}, u32[]{:S(2)}) collective-permute-start(f32[2,4,4,48]{3,2,1,0:T(4,128)S(1)} %get-tuple-element.86), channel_id=1, source_target_pairs={{0,1},{1,2},{2,3},{3,4},{4,5},{5,6},{6,7},{7,0},{8,9},{9,10},{10,1... | collective-permute-start | bytes 18440 | tf_op jit(solution)/shard_map/ppermute | solution.py:88
  65.5 5.9 %collective-permute-start.4 = (f32[2,4,4,48]{3,2,1,0:T(4,128)S(1)}, f32[2,4,4,48]{3,2,1,0:T(4,128)S(1)}, u32[]{:S(2)}, u32[]{:S(2)}) collective-permute-start(f32[2,4,4,48]{3,2,1,0:T(4,128)S(1)} %get-tuple-element.85), channel_id=1, source_target_pairs={{0,2},{1,3},{2,4},{3,5},{4,6},{5,7},{6,0},{7,1},{8,10},{9,11},{10,... | collective-permute-start | bytes 18440 | tf_op jit(solution)/shard_map/ppermute | solution.py:88
  65.5 6.3 %collective-permute-start.5 = (f32[2,4,4,48]{3,2,1,0:T(4,128)S(1)}, f32[2,4,4,48]{3,2,1,0:T(4,128)S(1)}, u32[]{:S(2)}, u32[]{:S(2)}) collective-permute-start(f32[2,4,4,48]{3,2,1,0:T(4,128)S(1)} %get-tuple-element.84), channel_id=1, source_target_pairs={{0,3},{1,4},{2,5},{3,6},{4,7},{5,0},{6,1},{7,2},{8,11},{9,12},{10,... | collective-permute-start | bytes 18440 | tf_op jit(solution)/shard_map/ppermute | solution.py:88
  68.2 4.4 %collective-permute-start.6 = (f32[2,4,4,48]{3,2,1,0:T(4,128)S(1)}, f32[2,4,4,48]{3,2,1,0:T(4,128)S(1)}, u32[]{:S(2)}, u32[]{:S(2)}) collective-permute-start(f32[2,4,4,48]{3,2,1,0:T(4,128)S(1)} %get-tuple-element.83), channel_id=1, source_target_pairs={{0,4},{1,5},{2,6},{3,7},{4,0},{5,1},{6,2},{7,3},{8,12},{9,13},{10,... | collective-permute-start | bytes 18440 | tf_op jit(solution)/shard_map/ppermute | solution.py:88
  68.8 4.7 %collective-permute-start.7 = (f32[2,4,4,48]{3,2,1,0:T(4,128)S(1)}, f32[2,4,4,48]{3,2,1,0:T(4,128)S(1)}, u32[]{:S(2)}, u32[]{:S(2)}) collective-permute-start(f32[2,4,4,48]{3,2,1,0:T(4,128)S(1)} %get-tuple-element.82), channel_id=1, source_target_pairs={{0,5},{1,6},{2,7},{3,0},{4,1},{5,2},{6,3},{7,4},{8,13},{9,14},{10,... | collective-permute-start | bytes 18440 | tf_op jit(solution)/shard_map/ppermute | solution.py:88
  71.0 2.6 collective-permute-start.8
  71.4 3.6 %collective-permute-start.9 = (f32[2,4,4,48]{3,2,1,0:T(4,128)S(1)}, f32[2,4,4,48]{3,2,1,0:T(4,128)S(1)}, u32[]{:S(2)}, u32[]{:S(2)}) collective-permute-start(f32[2,4,4,48]{3,2,1,0:T(4,128)S(1)} %get-tuple-element.80), channel_id=1, source_target_pairs={{0,7},{1,0},{2,1},{3,2},{4,3},{5,4},{6,5},{7,6},{8,15},{9,8},{10,9... | collective-permute-start | bytes 18440 | tf_op jit(solution)/shard_map/ppermute | solution.py:88
  89.4 16.9 %copy-start.4 = (f32[2,4,32,384]{3,2,1,0:T(8,128)}, f32[2,4,32,384]{3,2,1,0:T(8,128)S(1)}, u32[]{:S(2)}) copy-start(f32[2,4,32,384]{3,2,1,0:T(8,128)S(1)} %copy.54) | copy-start | bytes 1179652
  89.4 12.5 %collective-permute-start.10 = (f32[2,4,32,384]{3,2,1,0:T(8,128)S(1)}, f32[2,4,32,384]{3,2,1,0:T(8,128)S(1)}, u32[]{:S(2)}, u32[]{:S(2)}) collective-permute-start(f32[2,4,32,384]{3,2,1,0:T(8,128)S(1)} %copy.54), channel_id=1, source_target_pairs={{0,64},{64,128},{128,192},{1,65},{65,129},{129,193},{2,66},{66,130... | collective-permute-start | bytes 1179656 | tf_op jit(solution)/shard_map/ppermute | solution.py:23
  102.7 13.7 %collective-permute-start.11 = (f32[4,1,32,384]{3,2,1,0:T(8,128)}, f32[4,1,32,384]{3,2,1,0:T(8,128)S(1)}, u32[]{:S(2)}, u32[]{:S(2)}) collective-permute-start(f32[4,1,32,384]{3,2,1,0:T(8,128)} %get-tuple-element.65), channel_id=1, source_target_pairs={{0,8},{8,16},{16,24},{24,32},{32,40},{40,48},{48,56},{1,9},{9,17},... | collective-permute-start | bytes 589832 | tf_op jit(solution)/shard_map/ppermute | solution.py:34
  106.3 10.2 %collective-permute-start.12 = (f32[4,1,32,384]{3,2,1,0:T(8,128)}, f32[4,1,32,384]{3,2,1,0:T(8,128)}, u32[]{:S(2)}, u32[]{:S(2)}) collective-permute-start(f32[4,1,32,384]{3,2,1,0:T(8,128)} %get-tuple-element.66), channel_id=1, source_target_pairs={{8,0},{16,8},{24,16},{32,24},{40,32},{48,40},{56,48},{9,1},{17,9},... | collective-permute-start | bytes 589832 | tf_op jit(solution)/shard_map/ppermute | solution.py:36
  127.1 15.3 %copy-start.9 = (f32[2,4,4,384]{3,2,1,0:T(4,128)S(1)}, f32[2,4,4,384]{3,2,1,0:T(4,128)}, u32[]{:S(2)}) copy-start(f32[2,4,4,384]{3,2,1,0:T(4,128)} %param.13) | copy-start | bytes 147460
  127.1 15.3 %copy-start.11 = (f32[384]{0:T(512)S(1)}, f32[384]{0:T(512)}, u32[]{:S(2)}) copy-start(f32[384]{0:T(512)} %param.19) | copy-start | bytes 4612
  127.1 15.4 %copy-start.13 = (f32[384]{0:T(512)S(1)}, f32[384]{0:T(512)}, u32[]{:S(2)}) copy-start(f32[384]{0:T(512)} %param.20) | copy-start | bytes 4612
  127.1 16.6 %copy-start.6 = (f32[384,384]{1,0:T(8,128)S(1)}, f32[384,384]{1,0:T(8,128)}, u32[]{:S(2)}) copy-start(f32[384,384]{1,0:T(8,128)} %param.23) | copy-start | bytes 1769476
  127.2 17.7 %copy-start.7 = (f32[384,384]{1,0:T(8,128)S(1)}, f32[384,384]{1,0:T(8,128)}, u32[]{:S(2)}) copy-start(f32[384,384]{1,0:T(8,128)} %param.21) | copy-start | bytes 1769476
  130.5 7.8 %collective-permute-start.13 = (f32[2,4,4,48]{3,2,1,0:T(4,128)S(1)}, f32[2,4,4,48]{3,2,1,0:T(4,128)S(1)}, u32[]{:S(2)}, u32[]{:S(2)}) collective-permute-start(f32[2,4,4,48]{3,2,1,0:T(4,128)S(1)} %get-tuple-element.79), channel_id=1, source_target_pairs={{0,1},{1,2},{2,3},{3,4},{4,5},{5,6},{6,7},{7,0},{8,9},{9,10},{10,1... | collective-permute-start | bytes 18440 | tf_op jit(solution)/shard_map/ppermute | solution.py:88
  131.5 6.8 %collective-permute-start.14 = (f32[2,4,4,48]{3,2,1,0:T(4,128)S(1)}, f32[2,4,4,48]{3,2,1,0:T(4,128)S(1)}, u32[]{:S(2)}, u32[]{:S(2)}) collective-permute-start(f32[2,4,4,48]{3,2,1,0:T(4,128)S(1)} %get-tuple-element.78), channel_id=1, source_target_pairs={{0,2},{1,3},{2,4},{3,5},{4,6},{5,7},{6,0},{7,1},{8,10},{9,11},{10,... | collective-permute-start | bytes 18440 | tf_op jit(solution)/shard_map/ppermute | solution.py:88
  132.7 6.5 %collective-permute-start.15 = (f32[2,4,4,48]{3,2,1,0:T(4,128)S(1)}, f32[2,4,4,48]{3,2,1,0:T(4,128)S(1)}, u32[]{:S(2)}, u32[]{:S(2)}) collective-permute-start(f32[2,4,4,48]{3,2,1,0:T(4,128)S(1)} %get-tuple-element.77), channel_id=1, source_target_pairs={{0,3},{1,4},{2,5},{3,6},{4,7},{5,0},{6,1},{7,2},{8,11},{9,12},{10,... | collective-permute-start | bytes 18440 | tf_op jit(solution)/shard_map/ppermute | solution.py:88
  134.5 4.7 %collective-permute-start.16 = (f32[2,4,4,48]{3,2,1,0:T(4,128)S(1)}, f32[2,4,4,48]{3,2,1,0:T(4,128)S(1)}, u32[]{:S(2)}, u32[]{:S(2)}) collective-permute-start(f32[2,4,4,48]{3,2,1,0:T(4,128)S(1)} %get-tuple-element.76), channel_id=1, source_target_pairs={{0,4},{1,5},{2,6},{3,7},{4,0},{5,1},{6,2},{7,3},{8,12},{9,13},{10,... | collective-permute-start | bytes 18440 | tf_op jit(solution)/shard_map/ppermute | solution.py:88
  135.7 4.7 %collective-permute-start.17 = (f32[2,4,4,48]{3,2,1,0:T(4,128)S(1)}, f32[2,4,4,48]{3,2,1,0:T(4,128)S(1)}, u32[]{:S(2)}, u32[]{:S(2)}) collective-permute-start(f32[2,4,4,48]{3,2,1,0:T(4,128)S(1)} %get-tuple-element.75), channel_id=1, source_target_pairs={{0,5},{1,6},{2,7},{3,0},{4,1},{5,2},{6,3},{7,4},{8,13},{9,14},{10,... | collective-permute-start | bytes 18440 | tf_op jit(solution)/shard_map/ppermute | solution.py:88
  138.3 3.0 collective-permute-start.18
  138.3 3.2 %collective-permute-start.19 = (f32[2,4,4,48]{3,2,1,0:T(4,128)S(1)}, f32[2,4,4,48]{3,2,1,0:T(4,128)S(1)}, u32[]{:S(2)}, u32[]{:S(2)}) collective-permute-start(f32[2,4,4,48]{3,2,1,0:T(4,128)S(1)} %get-tuple-element.73), channel_id=1, source_target_pairs={{0,7},{1,0},{2,1},{3,2},{4,3},{5,4},{6,5},{7,6},{8,15},{9,8},{10,9... | collective-permute-start | bytes 18440 | tf_op jit(solution)/shard_map/ppermute | solution.py:88
  143.7 161.2 %all-gather.5.cloned.1.call-start = ((), (), s32[]{:S(2)}) async-start(), calls=%async_computation.1 | async-start | bytes 3194880 | tf_op jit(solution)/shard_map/all_gather | solution.py:146
  145.3 163.1 %copy-start.8 = (f32[384,384]{1,0:T(8,128)S(1)}, f32[384,384]{1,0:T(8,128)}, u32[]{:S(2)}) copy-start(f32[384,384]{1,0:T(8,128)} %param.24) | copy-start | bytes 1769476
  145.3 163.1 %copy-start.12 = (f32[384]{0:T(512)S(1)}, f32[384]{0:T(512)}, u32[]{:S(2)}) copy-start(f32[384]{0:T(512)} %param.25) | copy-start | bytes 4612
  (5 other events, 14.9 us)
Sparse Core Ops, SparseCore 0:
  143.8 82.4 all-gather.2
  229.0 75.7 all-gather.4
